TPU v7x, 512 devices: a whole 4x8x8 slice. The times are simulated.
512 devices in a mesh: row: 16 (over z, core), col: 32 (over y, x).
Axes of the slice: x: 4, y: 8, z: 8, core: 2. Of those that a mesh axis runs over, the one named last changes fastest.
Arguments:
- train_embed: bfloat16 [8192, 256], P(('row', 'col')), may hold values from -16 to 16
- valid_embed: bfloat16 [65536, 256], P(('row', 'col')), may hold values from -16 to 16
- train_labels: int32 [8192], P(('row', 'col')), may hold values from 0 to 99
- valid_labels: int32 [65536], P(('row', 'col')), may hold values from 0 to 99
- pair_level: int32 [100, 100], replicated, may hold values from 0 to 3
- level_cost: float32 [4], replicated, may hold values from 0.05 to 1
Outputs:
- calibrated: float32 [8192], P('row')
All inputs are finite; a program needn't handle non-finite values.
Results may differ from a plain program's by a relative error of at most 0.0003.
Values may be sent and summed in bfloat16 or wider, within the bound.
No kernel may reach another device: no remote copies, remote signals or barrier semaphores. Data moves between devices by JAX's collectives and lax.ppermute only.
A program may use at most 64 MiB of HBM per device.

v0:
```python
import math
import jax
import jax.numpy as jnp
from jax import lax
from jax.sharding import PartitionSpec as P

ITERS = 4
entropy_scale = 0.05


def inner_products(left_rows, right_rows):
    return lax.dot_general(
        left_rows, right_rows, (((1,), (1,)), ((), ())), preferred_element_type=jnp.float32
    )


def squared_norms(embeddings):
    widened = embeddings.astype(jnp.float32)
    return jnp.sum(widened * widened, axis=1)


def class_costs(pair_level, level_cost):
    num_levels = level_cost.shape[0]
    selected = (
        pair_level[:, :, None] == jnp.arange(num_levels, dtype=jnp.int32)[None, None, :]
    ).astype(jnp.float32)
    return jnp.sum(selected * level_cost[None, None, :], axis=2)


def label_costs(row_labels, class_ids, labels_y):
    col_hot = (class_ids[:, None] == labels_y[None, :]).astype(jnp.float32)
    return jnp.dot(
        row_labels, col_hot, precision=lax.Precision.HIGHEST, preferred_element_type=jnp.float32
    )


def shards(train_embed, valid_embed, train_labels, valid_labels, pair_level, level_cost):
    rows_x, labels_x = (
        lax.all_gather(train_embed, "col", axis=0, tiled=True),
        lax.all_gather(train_labels, "col", axis=0, tiled=True),
    )
    width_d = rows_x.shape[1]
    classes = pair_level.shape[0]
    class_table = class_costs(pair_level, level_cost)
    class_ids = jnp.arange(classes, dtype=jnp.int32)
    train_hot = (labels_x[:, None] == class_ids[None, :]).astype(jnp.float32)
    row_labels = jnp.dot(
        train_hot, class_table, precision=lax.Precision.HIGHEST, preferred_element_type=jnp.float32
    )
    train_sq = squared_norms(rows_x)
    cols_y, labels_y = (
        lax.all_gather(valid_embed, "row", axis=0, tiled=True),
        lax.all_gather(valid_labels, "row", axis=0, tiled=True),
    )
    valid_sq = squared_norms(cols_y)
    label_full = label_costs(row_labels, class_ids, labels_y)

    def cost_block(offset, block_cols):
        block_y = lax.dynamic_slice_in_dim(cols_y, offset, block_cols, 0)
        block_sq = lax.dynamic_slice_in_dim(valid_sq, offset, block_cols, 0)
        label_slice = lax.dynamic_slice_in_dim(label_full, offset, block_cols, 1)
        return (
            train_sq[:, None] + block_sq[None, :] - 2.0 * inner_products(rows_x, block_y)
        ) / width_d + label_slice

    row_count = rows_x.shape[0]
    col_count = labels_y.shape[0]
    block_cols = min(512, col_count)
    block_count = col_count // block_cols
    block_ids = jnp.arange(block_count, dtype=jnp.int32)

    def scores(block_index, row_pot, col_pot):
        offset = block_index * block_cols
        cost_tile = cost_block(offset, block_cols)
        block_pot = lax.dynamic_slice_in_dim(col_pot, offset, block_cols, 0)
        return (
            (block_pot[None, :] - cost_tile) / entropy_scale,
            (row_pot[:, None] - cost_tile) / entropy_scale,
        )

    row_pot = jnp.zeros((row_count,), jnp.float32)
    col_pot = jnp.zeros((col_count,), jnp.float32)
    full_rows = row_count * lax.axis_size("row")
    full_cols = col_count * lax.axis_size("col")
    for iteration in range(ITERS):

        def local_peaks(running, block_index, row_pot=row_pot, col_pot=col_pot):
            row_side, col_side = scores(block_index, row_pot, col_pot)
            return (jnp.maximum(running, jnp.max(row_side, axis=1)), jnp.max(col_side, axis=0))

        row_local, col_local = lax.scan(
            local_peaks, jnp.full((row_count,), -jnp.inf, jnp.float32), block_ids
        )
        row_high = lax.pmax(row_local, "col")
        col_high = lax.pmax(col_local.reshape(col_count), "row")

        def local_totals(
            running,
            block_index,
            row_pot=row_pot,
            col_pot=col_pot,
            row_high=row_high,
            col_high=col_high,
        ):
            row_side, col_side = scores(block_index, row_pot, col_pot)
            block_high = lax.dynamic_slice_in_dim(col_high, block_index * block_cols, block_cols, 0)
            return (
                running + jnp.sum(jnp.exp(row_side - row_high[:, None]), axis=1),
                jnp.sum(jnp.exp(col_side - block_high[None, :]), axis=0),
            )

        row_part, col_part = lax.scan(local_totals, jnp.zeros((row_count,), jnp.float32), block_ids)
        row_sum = lax.psum(row_part, "col")
        col_sum = lax.psum(col_part.reshape(col_count), "row")
        row_new = entropy_scale * math.log(full_cols) - entropy_scale * (
            row_high + jnp.log(row_sum)
        )
        col_new = entropy_scale * math.log(full_rows) - entropy_scale * (
            col_high + jnp.log(col_sum)
        )
        row_pot = 0.5 * (row_pot + row_new)
        col_pot = 0.5 * (col_pot + col_new)
    potential_sum = lax.psum(jnp.sum(row_pot), "row")
    return (row_pot * full_rows - potential_sum) / (full_rows - 1)


def solution(mesh):
    placed = (
        P(("row", "col"), None),
        P(("row", "col"), None),
        P(("row", "col")),
        P(("row", "col")),
        P(),
        P(),
    )
    return jax.shard_map(shards, mesh=mesh, in_specs=placed, out_specs=P("row"), check_vma=False)
```

profile of v0, /device:TPU:1, one launch (start us, length us, event | category | flops | bytes accessed | tf_op | source)
XLA Modules:
  0.0 894.9 jit_solution(5116224132933514768)
XLA Ops:
  6.5 0.7 all-gather.3.cloned.1.call-update
  7.3 1.3 dynamic-slice
  9.4 0.9 dynamic-update-slice
  10.3 17.5 %all-reduce = s32[512]{0:T(512)S(1)} all-reduce(s32[512]{0:T(512)S(1)} %dynamic-update-slice), channel_id=1, replica_groups=mesh['row'=16,'col'=32] {'col'}, use_global_device_ids=true, to_apply=%add | all-reduce | flops 512 | bytes 4096
  27.7 28.0 %all-gather = s32[16,1,128]{2,1,0:T(1,128)S(1)} all-gather(s32[1,1,128]{2,1,0:T(1,128)} %bitcast.194), channel_id=1, replica_groups=mesh['row'=16,'col'=32] {'row'}, dimensions={0}, use_global_device_ids=true | all-gather | bytes 8704 | tf_op jit(solution)/shard_map/all_gather | solution.py:53
  55.7 34.7 %all_gather.12 = bf16[512,256]{1,0:T(8,128)(2,1)S(1)} all-gather(bf16[16,256]{1,0:T(8,128)(2,1)} %param.22), channel_id=1, replica_groups=mesh['row'=16,'col'=32] {'col'}, dimensions={0}, use_global_device_ids=true | all-gather | bytes 270336 | tf_op jit(solution)/shard_map/all_gather | solution.py:39
  90.5 1.1 select_reduce_fusion
  92.0 3.8 fusion.60
  95.8 1.6 multiply_reduce_fusion.4
  97.4 13.7 %while.100 = (s32[]{:T(128)}, f32[512]{0:T(512)S(1)}, f32[4,512]{1,0:T(4,128)S(1)}, f32[512]{0:T(512)S(1)}, s32[4]{0:T(128)S(1)}, /*index=5*/f32[2048]{0:T(1024)...) while((s32[]{:T(128)}, f32[512]{0:T(512)S(1)}, ...), condition=%wide.region_6.7_spmd.clone, body=%wide.region_3.6_spmd.clone.sunk | while | flops 136577024 | bytes 1596617 | solution.py:91
  98.9 1.9 fusion.89
  102.3 1.9 fusion.89
  105.7 1.9 fusion.89
  109.1 1.9 fusion.89
  111.1 36.0 %pmax.50 = f32[2048]{0:T(1024)S(1)} all-reduce(f32[2048]{0:T(1024)S(1)} %bitcast.188), channel_id=1, replica_groups=mesh['row'=16,'col'=32] {'row'}, use_global_device_ids=true, to_apply=%region_8.9 | all-reduce | flops 2048 | bytes 16384 | tf_op jit(solution)/shard_map/pmax | solution.py:95
  147.1 58.1 %pmax.49 = f32[512]{0:T(512)S(1)} all-reduce(f32[512]{0:T(512)S(1)} %get-tuple-element.462), channel_id=1, replica_groups=mesh['row'=16,'col'=32] {'col'}, use_global_device_ids=true, to_apply=%region_7.8 | all-reduce | flops 512 | bytes 4096 | tf_op jit(solution)/shard_map/pmax | solution.py:94
  205.2 14.1 %while.101 = (s32[]{:T(128)}, f32[512]{0:T(512)S(1)}, f32[4,512]{1,0:T(4,128)S(1)}, f32[512]{0:T(512)S(1)}, s32[4]{0:T(128)S(1)}, /*index=5*/f32[2048]{0:T(1024)...) while((s32[]{:T(128)}, f32[512]{0:T(512)S(1)}, ...), condition=%wide.region_12.13_spmd.clone, body=%wide.region_9.12_spmd.clone.sunk | while | flops 137101312 | bytes 1604829 | solution.py:112
  206.6 2.1 exponential_reduce_fusion.9
  210.1 2.1 exponential_reduce_fusion.9
  213.6 2.1 exponential_reduce_fusion.9
  217.1 2.1 exponential_reduce_fusion.9
  219.3 56.1 %psum.56 = f32[512]{0:T(512)S(1)} all-reduce(f32[512]{0:T(512)S(1)} %get-tuple-element.464), channel_id=1, replica_groups=mesh['row'=16,'col'=32] {'col'}, use_global_device_ids=true, to_apply=%region_13.14 | all-reduce | flops 512 | bytes 4096 | tf_op jit(solution)/shard_map/psum | solution.py:113
  275.5 51.8 %psum.57 = f32[2048]{0:T(1024)S(1)} all-reduce(f32[2048]{0:T(1024)S(1)} %bitcast.189), channel_id=1, replica_groups=mesh['row'=16,'col'=32] {'row'}, use_global_device_ids=true, to_apply=%region_14.15 | all-reduce | flops 2048 | bytes 16384 | tf_op jit(solution)/shard_map/psum | solution.py:114
  327.3 13.7 %while.102 = (s32[]{:T(128)}, f32[512]{0:T(512)S(1)}, f32[4,512]{1,0:T(4,128)S(1)}, s32[4]{0:T(128)S(1)}, f32[2048]{0:T(1024)S(1)}, /*index=5*/f32[512]{0:T(512)...) while((s32[]{:T(128)}, f32[512]{0:T(512)S(1)}, ...), condition=%wide.region_18.19_spmd.clone, body=%wide.region_15.18_spmd.clone.sunk | while | flops 137101312 | bytes 1604829 | solution.py:91
  328.7 2.0 multiply_reduce_fusion.9
  332.1 2.0 multiply_reduce_fusion.9
  335.5 2.0 multiply_reduce_fusion.9
  339.0 2.0 multiply_reduce_fusion.9
  341.0 24.0 %pmax.52 = f32[2048]{0:T(1024)S(1)} all-reduce(f32[2048]{0:T(1024)S(1)} %bitcast.190), channel_id=1, replica_groups=mesh['row'=16,'col'=32] {'row'}, use_global_device_ids=true, to_apply=%region_20.21 | all-reduce | flops 2048 | bytes 16384 | tf_op jit(solution)/shard_map/pmax | solution.py:95
  365.1 57.4 %pmax.51 = f32[512]{0:T(512)S(1)} all-reduce(f32[512]{0:T(512)S(1)} %get-tuple-element.466), channel_id=1, replica_groups=mesh['row'=16,'col'=32] {'col'}, use_global_device_ids=true, to_apply=%region_19.20 | all-reduce | flops 512 | bytes 4096 | tf_op jit(solution)/shard_map/pmax | solution.py:94
  422.5 14.9 %while.103 = (s32[]{:T(128)}, f32[512]{0:T(512)S(1)}, f32[4,512]{1,0:T(4,128)S(1)}, s32[4]{0:T(128)S(1)}, f32[2048]{0:T(1024)S(1)}, /*index=5*/f32[512]{0:T(512)...) while((s32[]{:T(128)}, f32[512]{0:T(512)S(1)}, ...), condition=%wide.region_24.25_spmd.clone, body=%wide.region_21.24_spmd.clone.sunk | while | flops 137625600 | bytes 1613041 | solution.py:112
  424.0 2.2 exponential_reduce_fusion.10
  427.7 2.2 exponential_reduce_fusion.10
  431.4 2.2 exponential_reduce_fusion.10
  435.2 2.2 exponential_reduce_fusion.10
  437.4 56.1 %psum.58 = f32[512]{0:T(512)S(1)} all-reduce(f32[512]{0:T(512)S(1)} %get-tuple-element.468), channel_id=1, replica_groups=mesh['row'=16,'col'=32] {'col'}, use_global_device_ids=true, to_apply=%region_25.26 | all-reduce | flops 512 | bytes 4096 | tf_op jit(solution)/shard_map/psum | solution.py:113
  493.6 51.8 %psum.59 = f32[2048]{0:T(1024)S(1)} all-reduce(f32[2048]{0:T(1024)S(1)} %bitcast.191), channel_id=1, replica_groups=mesh['row'=16,'col'=32] {'row'}, use_global_device_ids=true, to_apply=%region_26.27 | all-reduce | flops 2048 | bytes 16384 | tf_op jit(solution)/shard_map/psum | solution.py:114
  545.4 13.5 %while.104 = (s32[]{:T(128)}, f32[512]{0:T(512)S(1)}, f32[4,512]{1,0:T(4,128)S(1)}, s32[4]{0:T(128)S(1)}, f32[2048]{0:T(1024)S(1)}, /*index=5*/f32[512]{0:T(512)...) while((s32[]{:T(128)}, f32[512]{0:T(512)S(1)}, ...), condition=%wide.region_30.31_spmd.clone, body=%wide.region_27.30_spmd.clone.sunk | while | flops 137101312 | bytes 1604829 | solution.py:91
  546.7 2.0 multiply_reduce_fusion.10
  550.1 2.0 multiply_reduce_fusion.10
  553.4 2.0 multiply_reduce_fusion.10
  556.8 2.0 multiply_reduce_fusion.10
  558.8 24.1 %pmax.54 = f32[2048]{0:T(1024)S(1)} all-reduce(f32[2048]{0:T(1024)S(1)} %bitcast.192), channel_id=1, replica_groups=mesh['row'=16,'col'=32] {'row'}, use_global_device_ids=true, to_apply=%region_32.33 | all-reduce | flops 2048 | bytes 16384 | tf_op jit(solution)/shard_map/pmax | solution.py:95
  582.9 57.4 %pmax.53 = f32[512]{0:T(512)S(1)} all-reduce(f32[512]{0:T(512)S(1)} %get-tuple-element.470), channel_id=1, replica_groups=mesh['row'=16,'col'=32] {'col'}, use_global_device_ids=true, to_apply=%region_31.32 | all-reduce | flops 512 | bytes 4096 | tf_op jit(solution)/shard_map/pmax | solution.py:94
  640.3 15.5 %while.105 = (s32[]{:T(128)}, f32[512]{0:T(512)S(1)}, f32[4,512]{1,0:T(4,128)S(1)}, s32[4]{0:T(128)S(1)}, f32[2048]{0:T(1024)S(1)}, /*index=5*/f32[512]{0:T(512)...) while((s32[]{:T(128)}, f32[512]{0:T(512)S(1)}, ...), condition=%wide.region_36.37_spmd.clone, body=%wide.region_33.36_spmd.clone.sunk | while | flops 137625600 | bytes 1613041 | solution.py:112
  641.9 2.2 exponential_reduce_fusion.11
  645.8 2.2 exponential_reduce_fusion.11
  649.7 2.2 exponential_reduce_fusion.11
  653.5 2.2 exponential_reduce_fusion.11
  655.8 38.2 %psum.61 = f32[2048]{0:T(1024)S(1)} all-reduce(f32[2048]{0:T(1024)S(1)} %bitcast.193), channel_id=1, replica_groups=mesh['row'=16,'col'=32] {'row'}, use_global_device_ids=true, to_apply=%region_38.39 | all-reduce | flops 2048 | bytes 16384 | tf_op jit(solution)/shard_map/psum | solution.py:114
  694.1 13.1 %while.106 = (s32[]{:T(128)}, f32[512]{0:T(512)S(1)}, s32[4]{0:T(128)S(1)}, f32[2048]{0:T(1024)S(1)}, f32[512]{0:T(512)S(1)}, /*index=5*/f32[2048]{0:T(1024)S(1)...) while((s32[]{:T(128)}, f32[512]{0:T(512)S(1)}, ...), condition=%wide.region_41.42_spmd.clone, body=%wide.region_39.41_spmd.clone.sunk | while | flops 136315392 | bytes 1596617 | solution.py:91
  695.6 1.8 fusion.97
  698.9 1.8 fusion.97
  702.1 1.8 fusion.97
  705.4 1.8 fusion.97
  707.3 55.7 %pmax.55 = f32[512]{0:T(512)S(1)} all-reduce(f32[512]{0:T(512)S(1)} %get-tuple-element.474), channel_id=1, replica_groups=mesh['row'=16,'col'=32] {'col'}, use_global_device_ids=true, to_apply=%region_42.43 | all-reduce | flops 512 | bytes 4096 | tf_op jit(solution)/shard_map/pmax | solution.py:94
  763.0 13.4 %while.107 = (s32[]{:T(128)}, f32[512]{0:T(512)S(1)}, s32[4]{0:T(128)S(1)}, f32[2048]{0:T(1024)S(1)}, f32[512]{0:T(512)S(1)}, /*index=5*/f32[2048]{0:T(1024)S(1)...) while((s32[]{:T(128)}, f32[512]{0:T(512)S(1)}, ...), condition=%wide.region_45.46_spmd.clone, body=%wide.region_43.45_spmd.clone.sunk | while | flops 136577536 | bytes 1598673 | solution.py:112
  764.4 1.9 fusion.100
  767.7 1.9 fusion.100
  771.1 1.9 fusion.100
  774.4 1.9 fusion.100
  776.4 57.7 %all-reduce.1 = (f32[512]{0:T(512)S(1)}, f32[512]{0:T(512)S(1)}) all-reduce(f32[512]{0:T(512)S(1)} %get-tuple-element.475, f32[512]{0:T(512)S(1)} %get-tuple-element.472), channel_id=1, replica_groups=mesh['row'=16,'col'=32] {'col'}, use_global_device_ids=true, to_apply=%region_46.47 | all-reduce | flops 1024 | bytes 8192 | tf_op jit(solution)/shard_map/psum | solution.py:113
  834.7 52.1 %psum.63 = f32[]{:T(128)} all-reduce(f32[]{:T(128)} %get-tuple-element.1210), channel_id=1, replica_groups=mesh['row'=16,'col'=32] {'row'}, use_global_device_ids=true, to_apply=%region_48.49 | all-reduce | flops 1 | bytes 8 | tf_op jit(solution)/shard_map/psum | solution.py:123
  886.8 1.3 subtract_multiply_fusion.1
  (195 shorter events, 27.9 us)
Async XLA Ops:
  6.5 89.3 %all-gather.3.cloned.1.call-start = ((), (), s32[]{:S(2)}) async-start(), calls=%async_computation | async-start | bytes 1114112 | tf_op jit(solution)/shard_map/all_gather | solution.py:52
Sparse Core Ops, SparseCore 0:
  9.5 48.0 all-gather.2
where the time goes:
time: 897 us; the launch traced here: 895 us
  blocking collectives  757 us (84%)
  matrix products  68.1 us (8%)
  local copies, waits for them, and re-layouts  28.5 us (3%)
  loops' own time  21.2 us (2%)
  between operations  14.4 us (2%)
    pmax x4, blocking collectives, shards(): row_high = lax.pmax(row_local, 'col')  229 us
    psum x3, blocking collectives, shards(): row_sum = lax.psum(row_part, 'col')  170 us
    psum x3, blocking collectives, shards(): col_sum = lax.psum(col_part.reshape(col_count), 'row')  142 us
    pmax x3, blocking collectives, shards(): col_high = lax.pmax(col_local.reshape(col_count), 'row')  84.1 us
    dot_general x32, matrix products, inner_products(): lax.dot_general(left_rows, right_rows, (((1,), (1,)), ((), ())), preferre...  64 us
    psum x1, blocking collectives, shards(): potential_sum = lax.psum(jnp.sum(row_pot), 'row')  52.1 us
    all_gather x1, blocking collectives, shards(): lax.all_gather(train_embed, 'col', axis=0, tiled=True)  34.7 us
    all_gather x1, blocking collectives, shards(): lax.all_gather(valid_labels, 'row', axis=0, tiled=True)  28 us
  transfers between devices with their start and end apart: 1, of which 0 were waited for; matrix products, arithmetic and copies ran while one was open for 1% of the time, Pallas kernels for 0%

commit v1 on v0

--- a/solution.py
+++ b/solution.py
@@ -36,7 +36,12 @@
 
 def shards(train_embed, valid_embed, train_labels, valid_labels, pair_level, level_cost):
     rows_x, labels_x = (
-        lax.all_gather(train_embed, "col", axis=0, tiled=True),
+        jnp.concatenate(
+            lax.all_to_all(
+                jnp.stack([train_embed for _ in range(lax.axis_size("col"))]), "col", 0, 0
+            ),
+            0,
+        ),
         lax.all_gather(train_labels, "col", axis=0, tiled=True),
     )
     width_d = rows_x.shape[1]

time: 897 us -> 859 us (0.958)
  blocking collectives: 757 us -> 707 us
  starting transfers between devices: 0.01 us -> 10.5 us
    all_gather x1 -> x0, blocking collectives: 34.7 us -> none  [shards(): lax.all_gather(train_embed, 'col', axis=0, tiled=True)]
    pmax x3, blocking collectives: 84.1 us -> 71.7 us  [shards(): col_high = lax.pmax(col_local.reshape(col_count), 'row')]
    all_to_all x0 -> x1, starting transfers between devices: none -> 10.5 us  [shards(): lax.all_to_all(jnp.stack([train_embed for _ in range(lax.axis_size('col')...]
  transfers between devices with their start and end apart: 1 -> 2, of which waited for: 0 -> 0; matrix products, arithmetic and copies ran while one was open for 1% -> 1% of each run, Pallas kernels for 0% -> 0%
where the time goes in v1:
time: 859 us; the launch traced here: 857 us
  blocking collectives  707 us (82%)
  matrix products  68.1 us (8%)
  local copies, waits for them, and re-layouts  29.7 us (3%)
  loops' own time  21.4 us (2%)
  between operations  14.4 us (2%)
  starting transfers between devices  10.5 us (1%)
    pmax x4, blocking collectives, shards(): row_high = lax.pmax(row_local, 'col')  226 us
    psum x3, blocking collectives, shards(): row_sum = lax.psum(row_part, 'col')  171 us
    psum x3, blocking collectives, shards(): col_sum = lax.psum(col_part.reshape(col_count), 'row')  142 us
    pmax x3, blocking collectives, shards(): col_high = lax.pmax(col_local.reshape(col_count), 'row')  71.7 us
    dot_general x32, matrix products, inner_products(): lax.dot_general(left_rows, right_rows, (((1,), (1,)), ((), ())), preferre...  63.9 us
    psum x1, blocking collectives, shards(): potential_sum = lax.psum(jnp.sum(row_pot), 'row')  52.1 us
    all_gather x1, blocking collectives, shards(): lax.all_gather(valid_labels, 'row', axis=0, tiled=True)  27.9 us
    dynamic_slice x32, local copies, waits for them, and re-layouts, shards(): lax.scan(local_peaks, jnp.full((row_count,), -jnp.inf, jnp.float32), bloc...  19.6 us
  transfers between devices with their start and end apart: 2, of which 0 were waited for; matrix products, arithmetic and copies ran while one was open for 1% of the time, Pallas kernels for 0%

profile of v1, /device:TPU:1, one launch (start us, length us, event | category | flops | bytes accessed | tf_op | source)
XLA Modules:
  0.0 857.4 jit_solution(4624202382016101675)
XLA Ops:
  7.3 1.4 stack.2
  8.7 10.5 %all-to-all-start = ((bf16[32,16,256]{2,1,0:T(8,128)(2,1)}), bf16[32,16,256]{2,1,0:T(8,128)(2,1)S(1)}, u32[]{:S(2)}, u32[]{:S(2)}) async-start(bf16[32,16,256]{2,1,0:T(8,128)(2,1)} %stack.2), calls=%async_computation | async-start | bytes 524288 | tf_op jit(solution)/shard_map/all_to_all | solution.py:40
  19.3 1.3 dynamic-slice
  21.3 0.9 dynamic-update-slice
  22.2 16.6 %all-reduce = s32[512]{0:T(512)S(1)} all-reduce(s32[512]{0:T(512)S(1)} %dynamic-update-slice), channel_id=1, replica_groups=mesh['row'=16,'col'=32] {'col'}, use_global_device_ids=true, to_apply=%add | all-reduce | flops 512 | bytes 4096
  38.7 27.9 %all-gather = s32[16,1,128]{2,1,0:T(1,128)S(1)} all-gather(s32[1,1,128]{2,1,0:T(1,128)} %bitcast.196), channel_id=1, replica_groups=mesh['row'=16,'col'=32] {'row'}, dimensions={0}, use_global_device_ids=true | all-gather | bytes 8704 | tf_op jit(solution)/shard_map/all_gather | solution.py:58
  66.7 1.0 select_reduce_fusion
  68.1 3.8 fusion.60
  72.1 1.6 multiply_reduce_fusion.4
  73.7 13.2 %while.100 = (s32[]{:T(128)}, f32[512]{0:T(512)S(1)}, f32[4,512]{1,0:T(4,128)S(1)}, f32[512]{0:T(512)S(1)}, s32[4]{0:T(128)S(1)}, /*index=5*/f32[2048]{0:T(1024)...) while((s32[]{:T(128)}, f32[512]{0:T(512)S(1)}, ...), condition=%wide.region_6.7_spmd.clone, body=%wide.region_3.6_spmd.clone.sunk | while | flops 136577024 | bytes 1596617 | solution.py:96
  75.1 1.9 fusion.89
  78.4 1.9 fusion.89
  81.7 1.9 fusion.89
  85.0 1.9 fusion.89
  87.0 23.6 %pmax.50 = f32[2048]{0:T(1024)S(1)} all-reduce(f32[2048]{0:T(1024)S(1)} %bitcast.190), channel_id=1, replica_groups=mesh['row'=16,'col'=32] {'row'}, use_global_device_ids=true, to_apply=%region_8.9 | all-reduce | flops 2048 | bytes 16384 | tf_op jit(solution)/shard_map/pmax | solution.py:100
  110.6 56.7 %pmax.49 = f32[512]{0:T(512)S(1)} all-reduce(f32[512]{0:T(512)S(1)} %get-tuple-element.462), channel_id=1, replica_groups=mesh['row'=16,'col'=32] {'col'}, use_global_device_ids=true, to_apply=%region_7.8 | all-reduce | flops 512 | bytes 4096 | tf_op jit(solution)/shard_map/pmax | solution.py:99
  167.3 14.4 %while.101 = (s32[]{:T(128)}, f32[512]{0:T(512)S(1)}, f32[4,512]{1,0:T(4,128)S(1)}, f32[512]{0:T(512)S(1)}, s32[4]{0:T(128)S(1)}, /*index=5*/f32[2048]{0:T(1024)...) while((s32[]{:T(128)}, f32[512]{0:T(512)S(1)}, ...), condition=%wide.region_12.13_spmd.clone, body=%wide.region_9.12_spmd.clone.sunk | while | flops 137101312 | bytes 1604829 | solution.py:117
  168.7 2.1 exponential_reduce_fusion.9
  172.3 2.1 exponential_reduce_fusion.9
  175.9 2.1 exponential_reduce_fusion.9
  179.5 2.1 exponential_reduce_fusion.9
  181.7 57.1 %psum.56 = f32[512]{0:T(512)S(1)} all-reduce(f32[512]{0:T(512)S(1)} %get-tuple-element.464), channel_id=1, replica_groups=mesh['row'=16,'col'=32] {'col'}, use_global_device_ids=true, to_apply=%region_13.14 | all-reduce | flops 512 | bytes 4096 | tf_op jit(solution)/shard_map/psum | solution.py:118
  238.8 51.8 %psum.57 = f32[2048]{0:T(1024)S(1)} all-reduce(f32[2048]{0:T(1024)S(1)} %bitcast.191), channel_id=1, replica_groups=mesh['row'=16,'col'=32] {'row'}, use_global_device_ids=true, to_apply=%region_14.15 | all-reduce | flops 2048 | bytes 16384 | tf_op jit(solution)/shard_map/psum | solution.py:119
  290.7 13.8 %while.102 = (s32[]{:T(128)}, f32[512]{0:T(512)S(1)}, f32[4,512]{1,0:T(4,128)S(1)}, s32[4]{0:T(128)S(1)}, f32[2048]{0:T(1024)S(1)}, /*index=5*/f32[512]{0:T(512)...) while((s32[]{:T(128)}, f32[512]{0:T(512)S(1)}, ...), condition=%wide.region_18.19_spmd.clone, body=%wide.region_15.18_spmd.clone.sunk | while | flops 137101312 | bytes 1604829 | solution.py:96
  292.1 2.0 multiply_reduce_fusion.9
  295.5 2.0 multiply_reduce_fusion.9
  299.0 2.0 multiply_reduce_fusion.9
  302.5 2.0 multiply_reduce_fusion.9
  304.5 24.1 %pmax.52 = f32[2048]{0:T(1024)S(1)} all-reduce(f32[2048]{0:T(1024)S(1)} %bitcast.192), channel_id=1, replica_groups=mesh['row'=16,'col'=32] {'row'}, use_global_device_ids=true, to_apply=%region_20.21 | all-reduce | flops 2048 | bytes 16384 | tf_op jit(solution)/shard_map/pmax | solution.py:100
  328.6 56.5 %pmax.51 = f32[512]{0:T(512)S(1)} all-reduce(f32[512]{0:T(512)S(1)} %get-tuple-element.466), channel_id=1, replica_groups=mesh['row'=16,'col'=32] {'col'}, use_global_device_ids=true, to_apply=%region_19.20 | all-reduce | flops 512 | bytes 4096 | tf_op jit(solution)/shard_map/pmax | solution.py:99
  385.1 15.0 %while.103 = (s32[]{:T(128)}, f32[512]{0:T(512)S(1)}, f32[4,512]{1,0:T(4,128)S(1)}, s32[4]{0:T(128)S(1)}, f32[2048]{0:T(1024)S(1)}, /*index=5*/f32[512]{0:T(512)...) while((s32[]{:T(128)}, f32[512]{0:T(512)S(1)}, ...), condition=%wide.region_24.25_spmd.clone, body=%wide.region_21.24_spmd.clone.sunk | while | flops 137625600 | bytes 1613041 | solution.py:117
  386.6 2.2 exponential_reduce_fusion.10
  390.3 2.2 exponential_reduce_fusion.10
  394.1 2.2 exponential_reduce_fusion.10
  397.9 2.2 exponential_reduce_fusion.10
  400.1 57.0 %psum.58 = f32[512]{0:T(512)S(1)} all-reduce(f32[512]{0:T(512)S(1)} %get-tuple-element.468), channel_id=1, replica_groups=mesh['row'=16,'col'=32] {'col'}, use_global_device_ids=true, to_apply=%region_25.26 | all-reduce | flops 512 | bytes 4096 | tf_op jit(solution)/shard_map/psum | solution.py:118
  457.1 51.8 %psum.59 = f32[2048]{0:T(1024)S(1)} all-reduce(f32[2048]{0:T(1024)S(1)} %bitcast.193), channel_id=1, replica_groups=mesh['row'=16,'col'=32] {'row'}, use_global_device_ids=true, to_apply=%region_26.27 | all-reduce | flops 2048 | bytes 16384 | tf_op jit(solution)/shard_map/psum | solution.py:119
  509.0 13.9 %while.104 = (s32[]{:T(128)}, f32[512]{0:T(512)S(1)}, f32[4,512]{1,0:T(4,128)S(1)}, s32[4]{0:T(128)S(1)}, f32[2048]{0:T(1024)S(1)}, /*index=5*/f32[512]{0:T(512)...) while((s32[]{:T(128)}, f32[512]{0:T(512)S(1)}, ...), condition=%wide.region_30.31_spmd.clone, body=%wide.region_27.30_spmd.clone.sunk | while | flops 137101312 | bytes 1604829 | solution.py:96
  510.4 2.0 multiply_reduce_fusion.10
  513.9 2.0 multiply_reduce_fusion.10
  517.3 2.0 multiply_reduce_fusion.10
  520.8 2.0 multiply_reduce_fusion.10
  522.9 24.1 %pmax.54 = f32[2048]{0:T(1024)S(1)} all-reduce(f32[2048]{0:T(1024)S(1)} %bitcast.194), channel_id=1, replica_groups=mesh['row'=16,'col'=32] {'row'}, use_global_device_ids=true, to_apply=%region_32.33 | all-reduce | flops 2048 | bytes 16384 | tf_op jit(solution)/shard_map/pmax | solution.py:100
  546.9 56.5 %pmax.53 = f32[512]{0:T(512)S(1)} all-reduce(f32[512]{0:T(512)S(1)} %get-tuple-element.470), channel_id=1, replica_groups=mesh['row'=16,'col'=32] {'col'}, use_global_device_ids=true, to_apply=%region_31.32 | all-reduce | flops 512 | bytes 4096 | tf_op jit(solution)/shard_map/pmax | solution.py:99
  603.4 15.0 %while.105 = (s32[]{:T(128)}, f32[512]{0:T(512)S(1)}, f32[4,512]{1,0:T(4,128)S(1)}, s32[4]{0:T(128)S(1)}, f32[2048]{0:T(1024)S(1)}, /*index=5*/f32[512]{0:T(512)...) while((s32[]{:T(128)}, f32[512]{0:T(512)S(1)}, ...), condition=%wide.region_36.37_spmd.clone, body=%wide.region_33.36_spmd.clone.sunk | while | flops 137625600 | bytes 1613041 | solution.py:117
  604.9 2.2 exponential_reduce_fusion.11
  608.7 2.2 exponential_reduce_fusion.11
  612.4 2.2 exponential_reduce_fusion.11
  616.2 2.2 exponential_reduce_fusion.11
  618.5 38.2 %psum.61 = f32[2048]{0:T(1024)S(1)} all-reduce(f32[2048]{0:T(1024)S(1)} %bitcast.195), channel_id=1, replica_groups=mesh['row'=16,'col'=32] {'row'}, use_global_device_ids=true, to_apply=%region_38.39 | all-reduce | flops 2048 | bytes 16384 | tf_op jit(solution)/shard_map/psum | solution.py:119
  656.8 13.0 %while.106 = (s32[]{:T(128)}, f32[512]{0:T(512)S(1)}, s32[4]{0:T(128)S(1)}, f32[2048]{0:T(1024)S(1)}, f32[512]{0:T(512)S(1)}, /*index=5*/f32[2048]{0:T(1024)S(1)...) while((s32[]{:T(128)}, f32[512]{0:T(512)S(1)}, ...), condition=%wide.region_41.42_spmd.clone, body=%wide.region_39.41_spmd.clone.sunk | while | flops 136315392 | bytes 1596617 | solution.py:96
  658.2 1.8 fusion.97
  661.4 1.8 fusion.97
  664.7 1.8 fusion.97
  667.9 1.8 fusion.97
  669.7 56.4 %pmax.55 = f32[512]{0:T(512)S(1)} all-reduce(f32[512]{0:T(512)S(1)} %get-tuple-element.474), channel_id=1, replica_groups=mesh['row'=16,'col'=32] {'col'}, use_global_device_ids=true, to_apply=%region_42.43 | all-reduce | flops 512 | bytes 4096 | tf_op jit(solution)/shard_map/pmax | solution.py:99
  726.1 13.4 %while.107 = (s32[]{:T(128)}, f32[512]{0:T(512)S(1)}, s32[4]{0:T(128)S(1)}, f32[2048]{0:T(1024)S(1)}, f32[512]{0:T(512)S(1)}, /*index=5*/f32[2048]{0:T(1024)S(1)...) while((s32[]{:T(128)}, f32[512]{0:T(512)S(1)}, ...), condition=%wide.region_45.46_spmd.clone, body=%wide.region_43.45_spmd.clone.sunk | while | flops 136577536 | bytes 1598673 | solution.py:117
  727.5 1.9 fusion.100
  730.9 1.9 fusion.100
  734.2 1.9 fusion.100
  737.6 1.9 fusion.100
  739.5 57.0 %all-reduce.1 = (f32[512]{0:T(512)S(1)}, f32[512]{0:T(512)S(1)}) all-reduce(f32[512]{0:T(512)S(1)} %get-tuple-element.475, f32[512]{0:T(512)S(1)} %get-tuple-element.472), channel_id=1, replica_groups=mesh['row'=16,'col'=32] {'col'}, use_global_device_ids=true, to_apply=%region_46.47 | all-reduce | flops 1024 | bytes 8192 | tf_op jit(solution)/shard_map/psum | solution.py:118
  797.2 52.1 %psum.63 = f32[]{:T(128)} all-reduce(f32[]{:T(128)} %get-tuple-element.1297), channel_id=1, replica_groups=mesh['row'=16,'col'=32] {'row'}, use_global_device_ids=true, to_apply=%region_48.49 | all-reduce | flops 1 | bytes 8 | tf_op jit(solution)/shard_map/psum | solution.py:128
  849.3 1.3 subtract_multiply_fusion.1
  (198 shorter events, 28.4 us)
Async XLA Ops:
  6.5 65.6 %all-gather.3.cloned.1.call-start = ((), (), s32[]{:S(2)}) async-start(), calls=%async_computation.1 | async-start | bytes 1114112 | tf_op jit(solution)/shard_map/all_gather | solution.py:57
  8.7 63.2 %all-to-all-start = ((bf16[32,16,256]{2,1,0:T(8,128)(2,1)}), bf16[32,16,256]{2,1,0:T(8,128)(2,1)S(1)}, u32[]{:S(2)}, u32[]{:S(2)}) async-start(bf16[32,16,256]{2,1,0:T(8,128)(2,1)} %stack.2), calls=%async_computation | async-start | bytes 524288 | tf_op jit(solution)/shard_map/all_to_all | solution.py:40
Sparse Core Ops, SparseCore 0:
  9.5 47.8 all-gather.2
